TPU v7x, 32 devices: a whole 2x2x4 slice. The times are simulated.
32 devices in a mesh: rep: 4 (over x, core), shard: 8 (over z, y).
Axes of the slice: x: 2, y: 2, z: 4, core: 2. Of those that a mesh axis runs over, the one named last changes fastest.
Arguments:
- tokens: bfloat16 [8192, 1536], P(('rep', 'shard')), may hold values from -6 to 6
- segments: int32 [32, 256], P(('rep', 'shard')), may hold values from 0 to 2, never falling along the last dimension, each value on 1 to 128 neighbouring positions
- routes: int32 [8192, 8], P(('rep', 'shard')), may hold values from 0 to 15, all different within a row; in each aligned block of 256 rows (0 to 255, 256 to 511, ...) at most 160 rows name the same one
- cotangent: bfloat16 [8192, 1536], P(('rep', 'shard')), may hold values from -6 to 6
- wqkv: float32 [1536, 2560], P('shard'), may hold values from -0.15625 to 0.15625
- wqkv_first: float32 [1536, 2560], P('shard')
- wqkv_second: float32 [1536, 2560], P('shard'), may hold values from 1720.32 to 6881.28
- wo: float32 [1536, 1536], P('shard'), may hold values from -1.25 to 1.25
- wo_first: float32 [1536, 1536], P('shard')
- wo_second: float32 [1536, 1536], P('shard'), may hold values from 6.22592 to 24.576
- router: float32 [1536, 16], P('shard'), may hold values from -0.078125 to 0.078125
- router_first: float32 [1536, 16], P('shard')
- router_second: float32 [1536, 16], P('shard'), may hold values from 27607.04 to 110592
- w_in: float32 [16, 1536, 1024], P(None, 'shard'), may hold values from -0.15625 to 0.15625
- w_in_first: float32 [16, 1536, 1024], P(None, 'shard')
- w_in_second: float32 [16, 1536, 1024], P(None, 'shard'), may hold values from 52.4288 to 212.992
- w_out: float32 [16, 512, 1536], P(None, 'shard'), may hold values from -1 to 1
- w_out_first: float32 [16, 512, 1536], P(None, 'shard')
- w_out_second: float32 [16, 512, 1536], P(None, 'shard'), may hold values from 1.212416 to 4.83328
- gains: float32 [2, 1536], P(None, 'shard'), may hold values from 0.5 to 1.5
- gains_first: float32 [2, 1536], P(None, 'shard')
- gains_second: float32 [2, 1536], P(None, 'shard'), may hold values from 1720.32 to 6881.28
Outputs:
- mixed: bfloat16 [8192, 1536], P(('rep', 'shard'))
- tokens_grad: float32 [8192, 1536], P(('rep', 'shard'))
- wqkv_first_new: float32 [1536, 2560], P('shard')
- wqkv_second_new: float32 [1536, 2560], P('shard')
- wqkv_new: float32 [1536, 2560], P('shard')
- wo_first_new: float32 [1536, 1536], P('shard')
- wo_second_new: float32 [1536, 1536], P('shard')
- wo_new: float32 [1536, 1536], P('shard')
- router_first_new: float32 [1536, 16], P('shard')
- router_second_new: float32 [1536, 16], P('shard')
- router_new: float32 [1536, 16], P('shard')
- w_in_first_new: float32 [16, 1536, 1024], P(None, 'shard')
- w_in_second_new: float32 [16, 1536, 1024], P(None, 'shard')
- w_in_new: float32 [16, 1536, 1024], P(None, 'shard')
- w_out_first_new: float32 [16, 512, 1536], P(None, 'shard')
- w_out_second_new: float32 [16, 512, 1536], P(None, 'shard')
- w_out_new: float32 [16, 512, 1536], P(None, 'shard')
- gains_first_new: float32 [2, 1536], P(None, 'shard')
- gains_second_new: float32 [2, 1536], P(None, 'shard')
- gains_new: float32 [2, 1536], P(None, 'shard')
Inputs may be any that keep to these rules, and one draw needn't show every extreme that they name: `segments`: numbers never fall along a sequence; a document holds 1 to half of 256 positions, and some document of each draw holds exactly half. `routes`: each token names 8 different experts; among the tokens of one sequence no expert is named more than 160 times, and in every draw some expert is named exactly 160 times in some sequence.
All inputs are finite; a program needn't handle non-finite values.
Results may differ from a plain program's by a relative error of at most 0.024.
Values may be sent and summed in bfloat16 or wider, within the bound.
A program may use at most 256 MiB of HBM per device.

v0:
```python
import functools

import jax
import jax.numpy as jnp
from jax import lax
from jax.experimental import pallas as pl
from jax.experimental.pallas import tpu as pltpu
from jax.sharding import PartitionSpec as P

D = 1536
H = 512
HEADS = 24
KV_HEADS = 8
HD = 64
E = 16
TOP = 8
STEP = 10
QD = 1536
KVD = 512
GROUP = 4

HIGH = lax.Precision.HIGHEST
MESH = pl.DeviceIdType.MESH
norm_eps = 1e-06
beta_one = 0.9
beta_two = 0.95
adam_eps = 1e-08
decay_rate = 0.1
masked_score = -1e30
HOOK = 0
OUT_STEPS = (0, 24, 24, 24)
EARLY = (1, 1, 1, 1)
VMEM_BYTES = 56 * 2**20
EXPERT_VMEM_BYTES = 62 * 2**20


def flip(index, bit):
    step = 2**bit
    return index + (1 - 2 * ((index // step) % 2)) * step


def moved(place, bits):
    rep, shard = place
    for axis, bit in bits:
        if axis == "r":
            rep = flip(rep, bit)
        else:
            shard = flip(shard, bit)
    return (rep, shard)


def subsets(bits):
    result = [()]
    for bit in bits:
        result = result + [item + (bit,) for item in result]
    return result


def here():
    return (lax.axis_index("rep"), lax.axis_index("shard"))


def meet(places):
    barrier = pltpu.get_barrier_semaphore()
    for place in places:
        pl.semaphore_signal(barrier, inc=1, device_id=place, device_id_type=MESH)
    pl.semaphore_wait(barrier, len(places))


def start_copy(source, target, sems, index, place):
    copy = pltpu.make_async_remote_copy(
        src_ref=source,
        dst_ref=target,
        send_sem=sems[0].at[index],
        recv_sem=sems[1].at[index],
        device_id=place,
        device_id_type=MESH,
    )
    copy.start()
    return copy


class Counter:
    def __init__(self):
        self.value = 0

    def next(self):
        self.value += 1
        return self.value - 1


def gather_flows(flows, me, sems, count, hooks=()):
    sends = []
    for _ in gather_steps(flows, me, sems, count, sends, hooks):
        pass
    return sends


def gather_steps(flows, me, sems, count, sends, hooks=()):
    plans = []
    for order, source, target, local in flows:
        index = {}
        for level, bit in enumerate(order):
            for bits in subsets(order[:level]):
                if not (bit[0] == "r" and local(bits) and local(bits + (bit,))):
                    index[(level, bits)] = count.next()
        plans.append(index)
    deepest = max(len(order) for order, _, _, _ in flows)

    def push(flow, number, level, bits, ready):
        order, source, target, local = flow
        if (level, bits) not in plans[number]:
            return
        place = moved(me, bits)
        origin = source(place) if ready else target(place, bits)
        goal = target(place, bits + (order[level],))
        slot = plans[number][(level, bits)]
        sends.append(start_copy(origin, goal, sems, slot, moved(me, (order[level],))))

    for level in range(deepest):
        for number, flow in enumerate(flows):
            order, source, target, local = flow
            if level < len(order):
                for bits in subsets(order[:level]):
                    if local(bits):
                        push(flow, number, level, bits, True)
    yield
    hooks = dict(hooks)
    if -1 in hooks:
        hooks[-1]()
    for level in range(deepest):
        for turn in range(2**level):
            for number, flow in enumerate(flows):
                order, source, target, local = flow
                if level >= len(order):
                    continue
                bits = subsets(order[:level])[turn]
                key = (level, bits)
                if key not in plans[number]:
                    continue
                full = bits + (order[level],)
                place = moved(me, full)
                slot = plans[number][key]
                pltpu.make_async_remote_copy(
                    src_ref=target(place, full),
                    dst_ref=target(place, full),
                    send_sem=sems[0].at[slot],
                    recv_sem=sems[1].at[slot],
                    device_id=moved(me, (order[level],)),
                    device_id_type=MESH,
                ).wait_recv()
                for later in range(level + 1, len(order)):
                    push(flow, number, later, full, False)
                yield
        if level in hooks:
            hooks[level]()


def gather_slots(orders):
    return sum(2 ** len(order) - 1 for order in orders)


def add_into(target, first, second, block):
    rows = first.shape[0]

    def body(index, carry):
        window = pl.ds(pl.multiple_of(index * block, block), block)
        target[window] = first[window] + second[window]
        return carry

    if rows == block:
        target[...] = first[...] + second[...]
    else:
        lax.fori_loop(0, rows // block, body, 0)


def halving_slots(length):
    return 2 ** (length - 1) + 2**length - 1


def sum_flows(flows, me, sems, local_sems, count, local_count):
    sends = []
    for _ in sum_steps(flows, me, sems, local_sems, count, local_count, sends):
        pass
    return sends


def sum_steps(flows, me, sems, local_sems, count, local_count, sends):
    loads = []
    plans = []
    for order, source, buffer, block in flows:
        size = len(order)
        held = subsets(order[1:][::-1])
        place_of = {frozenset(bits): i for i, bits in enumerate(held)}
        index, slots, base = {}, {}, len(held)
        for level in range(size):
            for bits in subsets(order[level + 1 :][::-1]):
                index[(level, frozenset(bits))] = count.next()
                slots[(level, frozenset(bits))] = base
                base += 1
        plans.append((place_of, index, slots))
    deepest = max(len(order) for order, _, _, _ in flows)

    def turns(order, level):
        names = subsets(order[level + 1 :][::-1])
        return names[::-1]

    for turn in range(2 ** (deepest - 1)):
        for number, (order, source, buffer, block) in enumerate(flows):
            names = turns(order, 0)
            if turn >= len(names):
                continue
            bits = names[turn]
            key = frozenset(bits)
            place_of, index, slots = plans[number]
            sends.append(
                start_copy(
                    source(moved(me, bits + (order[0],))),
                    buffer.at[slots[(0, key)]],
                    sems,
                    index[(0, key)],
                    moved(me, (order[0],)),
                )
            )
            load = pltpu.make_async_copy(
                source(moved(me, bits)), buffer.at[place_of[key]], local_sems.at[local_count.next()]
            )
            load.start()
            loads.append(((number, key), load))
    waiting = dict(loads)
    yield
    for level in range(deepest):
        for turn in range(2 ** (deepest - 1 - level)):
            for number, (order, source, buffer, block) in enumerate(flows):
                if level >= len(order):
                    continue
                names = turns(order, level)
                if turn >= len(names):
                    continue
                bits = names[turn]
                key = frozenset(bits)
                place_of, index, slots = plans[number]
                slot = index[(level, key)]
                landed = buffer.at[slots[(level, key)]]
                pltpu.make_async_remote_copy(
                    src_ref=landed,
                    dst_ref=landed,
                    send_sem=sems[0].at[slot],
                    recv_sem=sems[1].at[slot],
                    device_id=moved(me, (order[level],)),
                    device_id_type=MESH,
                ).wait_recv()
                if level == 0:
                    waiting[(number, key)].wait()
                kept = buffer.at[place_of[key]]
                add_into(kept, kept, landed, block)
                if level + 1 < len(order) and order[level + 1] in key:
                    after = key - {order[level + 1]}
                    sends.append(
                        start_copy(
                            kept,
                            buffer.at[slots[(level + 1, after)]],
                            sems,
                            index[(level + 1, after)],
                            moved(me, (order[level + 1],)),
                        )
                    )
                yield


def rms_norm(value, gain):
    scale = lax.rsqrt(jnp.mean(value * value, axis=-1, keepdims=True) + norm_eps)
    return value * scale * gain


def norm_back(value, gain, grad):
    scale = lax.rsqrt(jnp.mean(value * value, axis=-1, keepdims=True) + norm_eps)
    normal = value * scale
    grad_gain = jnp.sum(grad * normal, axis=0)
    inner = grad * gain
    grad_value = scale * (inner - normal * jnp.mean(inner * normal, axis=-1, keepdims=True))
    return (grad_value, grad_gain)


def angle_tables(length, width):
    halfway = width // 2
    freqs = 10000.0 ** (-jnp.arange(halfway, dtype=jnp.float32) / halfway)
    angles = jnp.arange(length, dtype=jnp.float32)[:, None] * freqs[None, :]
    return (jnp.cos(angles)[:, None, :], jnp.sin(angles)[:, None, :], halfway)


def rotary(value):
    cosine, sine, halfway = angle_tables(value.shape[0], value.shape[-1])
    first = value[..., :halfway]
    second = value[..., halfway:]
    return jnp.concatenate(
        [first * cosine - second * sine, second * cosine + first * sine], axis=-1
    )


def rotary_back(grad):
    cosine, sine, halfway = angle_tables(grad.shape[0], grad.shape[-1])
    first = grad[..., :halfway]
    second = grad[..., halfway:]
    return jnp.concatenate(
        [first * cosine + second * sine, second * cosine - first * sine], axis=-1
    )


def block_scores(rows, keys, segs):
    places = jnp.arange(keys.shape[0], dtype=jnp.int32)
    scores = jnp.einsum(
        "sgrd,tgd->grst", rows, keys, preferred_element_type=jnp.float32
    ) * rows.shape[-1] ** (-0.5)
    allowed = (places[:, None] >= places[None, :]) & (segs[:, None] == segs[None, :])
    return jnp.where(allowed, scores, masked_score)


def attend_forward(query, keys, values, segs):
    length = query.shape[0]
    block = min(length, 512)

    def one_block(index):
        scores = block_scores(query, keys, segs)
        top = jnp.max(scores, axis=-1, keepdims=True)
        lse = top + jnp.log(jnp.sum(jnp.exp(scores - top), axis=-1, keepdims=True))
        probs = jnp.exp(scores - lse).astype(jnp.bfloat16)
        output = jnp.einsum("grst,tgd->sgrd", probs, values, preferred_element_type=jnp.float32)
        return (output.astype(jnp.bfloat16), lse)

    outputs, lses = lax.map(one_block, jnp.arange(length // block))
    return (outputs.reshape(query.shape), lses)


def attend_backward(query, keys, values, segs, lses, grad_out):
    length = query.shape[0]
    block = min(length, 512)
    scale = query.shape[-1] ** (-0.5)

    def step(carry, item):
        grad_key, grad_value = carry
        index, lse = item
        probs = jnp.exp(block_scores(query, keys, segs) - lse)
        grad_value = grad_value + jnp.einsum(
            "grst,sgrd->tgd",
            probs.astype(jnp.bfloat16),
            grad_out,
            preferred_element_type=jnp.float32,
        )
        grad_probs = jnp.einsum(
            "sgrd,tgd->grst", grad_out, values, preferred_element_type=jnp.float32
        )
        grad_scores = (
            probs * (grad_probs - jnp.sum(grad_probs * probs, axis=-1, keepdims=True))
        ).astype(jnp.bfloat16)
        grad_rows = (
            jnp.einsum("grst,tgd->sgrd", grad_scores, keys, preferred_element_type=jnp.float32)
            * scale
        )
        grad_key = (
            grad_key
            + jnp.einsum("grst,sgrd->tgd", grad_scores, query, preferred_element_type=jnp.float32)
            * scale
        )
        return ((grad_key, grad_value), grad_rows)

    zeros = jnp.zeros(keys.shape, jnp.float32)
    (grad_key, grad_value), grad_query = lax.scan(
        step, (zeros, zeros), (jnp.arange(length // block), lses)
    )
    return (grad_query.reshape(query.shape), grad_key, grad_value)


def adamw(weight, first, second, grad, rate, decay):
    first_new = beta_one * first + (1.0 - beta_one) * grad
    second_new = beta_two * second + (1.0 - beta_two) * grad * grad
    first_fix = 1.0 - beta_one**STEP
    second_fix = 1.0 - beta_two**STEP
    update = first_new / first_fix / (jnp.sqrt(second_new / second_fix) + adam_eps)
    return (first_new, second_new, weight - rate * (update + decay * weight))


X_BIT, C_BIT, Y_BIT, Z_BIT = ("r", 1), ("r", 0), ("s", 0), ("s", 1)
TURNED = (
    (X_BIT, Y_BIT, Z_BIT),
    (Y_BIT, Z_BIT, X_BIT),
    (Z_BIT, X_BIT, Y_BIT),
)
SUM_TURNED = (
    (Y_BIT, Z_BIT, X_BIT),
    (Z_BIT, Y_BIT, X_BIT),
    (Y_BIT, Z_BIT, X_BIT),
)
X_LAST = (
    (Z_BIT, Y_BIT, X_BIT),
    (Z_BIT, Y_BIT, X_BIT),
    (Z_BIT, Y_BIT, X_BIT),
)


POSITIONS = [
    frozenset(bits)
    for bits in (
        (X_BIT, Y_BIT, Z_BIT),
        (X_BIT, Y_BIT),
        (X_BIT, Z_BIT),
        (Y_BIT, Z_BIT),
        (X_BIT,),
        (Y_BIT,),
        (Z_BIT,),
        (),
    )
]


def position(bits):
    return POSITIONS.index(frozenset(bits))


def far_bits(shards):
    return tuple(("s", i) for i in range(2, shards.bit_length() - 1))


def only_self(bits):
    return not bits


def same_shard(bits):
    return all(axis == "r" for axis, _ in bits)


def token_flows(source, target, orders):
    width = source.shape[-1] // len(orders)
    flows = []
    for number, order in enumerate(orders):
        columns = pl.ds(number * width, width)
        flows.append(
            (
                order,
                lambda place, columns=columns: source.at[:, columns],
                lambda place, bits, columns=columns: target.at[position(bits), :, columns],
                only_self,
            )
        )
    return flows


def share_flows(source, target, orders, reps):
    height = source.shape[0] // len(orders)
    width = source.shape[1] // reps
    flows = []

    def columns_of(place):
        return pl.ds(pl.multiple_of(place[0] * width, 128), width)

    for number, order in enumerate(orders):
        rows = pl.ds(number * height, height)
        flows.append(
            (
                order,
                lambda place, rows=rows: source.at[rows, columns_of(place)],
                lambda place, bits, rows=rows: target.at[place[1], rows, columns_of(place)],
                same_shard,
            )
        )
    return flows


def neighbours(me, bits):
    return [moved(me, (bit,)) for bit in bits]


def open_kernel(shards, reps, *refs):
    qkv, out, small, w_in, w_out, cot = refs[:6]
    qkv_all, out_all, small_all, in_all, down_all, cot_all = refs[6:12]
    send, recv, local = refs[12:]
    me = here()
    sems = (send, recv)
    far = far_bits(shards)
    bits = (Y_BIT, Z_BIT) + far
    partners = [moved(me, item) for item in subsets(bits)[1:]][::-1]
    meet(neighbours(me, (X_BIT, C_BIT)) + partners)
    count = Counter()
    own = me[1]
    here_copies = [
        (qkv, qkv_all.at[own]),
        (out, out_all.at[own]),
        (small, small_all.at[own]),
        (w_in.at[own % GROUP], in_all.at[1, own]),
        (w_out.at[own % GROUP], down_all.at[1, own]),
        (cot, cot_all.at[position(())]),
    ]
    for number, (source, target) in enumerate(here_copies):
        pltpu.make_async_copy(source, target, local.at[number]).start()
    sends = []
    orders = [far + order + (C_BIT,) for order in X_LAST]
    flows = share_flows(qkv, qkv_all, orders, reps) + share_flows(out, out_all, orders, reps)
    flows.append(
        (far + (Y_BIT, Z_BIT), lambda place: small, lambda place, bits: small_all.at[place[1]], only_self)
    )
    flows += token_flows(cot, cot_all, X_LAST)
    direct = []

    def send_experts(chosen):
        for place in chosen:
            for source, target in ((w_in, in_all), (w_out, down_all)):
                slot = count.next()
                sends.append(
                    start_copy(source.at[place[1] % GROUP], target.at[1, own], sems, slot, place)
                )
                direct.append((target, place[1], slot, place))

    hooks = {HOOK: functools.partial(send_experts, partners)}
    sends += gather_flows(flows, me, sems, count, hooks)
    twin = moved(me, (C_BIT,))
    for source, target in ((w_in, in_all), (w_out, down_all)):
        sends.append(
            start_copy(source.at[own % GROUP], target.at[0, own], sems, count.next(), twin)
        )
    passed = [(target, own, count.value - 2 + i) for i, target in enumerate((in_all, down_all))]
    for target, index, slot, place in direct:
        landed = target.at[1, index]
        pltpu.make_async_remote_copy(
            src_ref=landed,
            dst_ref=landed,
            send_sem=send.at[slot],
            recv_sem=recv.at[slot],
            device_id=place,
            device_id_type=MESH,
        ).wait_recv()
        slot = count.next()
        sends.append(start_copy(landed, target.at[0, index], sems, slot, twin))
        passed.append((target, index, slot))
    for target, index, slot in passed:
        landed = target.at[0, index]
        pltpu.make_async_remote_copy(
            src_ref=landed,
            dst_ref=landed,
            send_sem=send.at[slot],
            recv_sem=recv.at[slot],
            device_id=twin,
            device_id_type=MESH,
        ).wait_recv()
    for copy in sends:
        copy.wait_send()
    for number, (source, target) in enumerate(here_copies):
        pltpu.make_async_copy(source, target, local.at[number]).wait()


def anywhere(count):
    return [pl.BlockSpec(memory_space=pl.ANY)] * count


def open_call(qkv, out, small, w_in, w_out, cot, shards, reps):
    def grown(array):
        return jax.ShapeDtypeStruct((shards,) + array.shape[-2:], array.dtype)

    shapes = [grown(array) for array in (qkv, out, small)]
    shapes += [
        jax.ShapeDtypeStruct((2, shards) + array.shape[1:], array.dtype) for array in (w_in, w_out)
    ]
    shapes.append(jax.ShapeDtypeStruct((len(POSITIONS),) + cot.shape, cot.dtype))
    slots = 6 * (shards * reps - 1) + shards + 4 * shards + 3 * 7
    return pl.pallas_call(
        functools.partial(open_kernel, shards, reps),
        out_shape=shapes,
        in_specs=anywhere(6),
        out_specs=anywhere(6),
        scratch_shapes=[
            pltpu.SemaphoreType.DMA((slots,)),
            pltpu.SemaphoreType.DMA((slots,)),
            pltpu.SemaphoreType.DMA((6,)),
        ],
        compiler_params=pltpu.CompilerParams(
            collective_id=0, has_side_effects=True, vmem_limit_bytes=VMEM_BYTES
        ),
        name="open_gather",
    )(qkv, out, small, w_in, w_out, cot)


def spread_kernel(*refs):
    rows, gate, rows_all, gate_all, send, recv, local = refs
    me = here()
    sems = (send, recv)
    meet(neighbours(me, (X_BIT, Y_BIT, Z_BIT)))
    count = Counter()
    copies = [
        (rows, rows_all.at[position(())]),
        (gate, gate_all.at[position(())]),
    ]
    for number, (source, target) in enumerate(copies):
        pltpu.make_async_copy(source, target, local.at[number]).start()
    flows = token_flows(rows, rows_all, TURNED)
    flows.append(
        (
            TURNED[0],
            lambda place: gate,
            lambda place, bits: gate_all.at[position(bits)],
            only_self,
        )
    )
    for copy in gather_flows(flows, me, sems, count):
        copy.wait_send()
    for number, (source, target) in enumerate(copies):
        pltpu.make_async_copy(source, target, local.at[number]).wait()


def spread_call(rows, gate):
    slots = 4 * 7
    return pl.pallas_call(
        spread_kernel,
        out_shape=[
            jax.ShapeDtypeStruct((len(POSITIONS),) + array.shape, array.dtype)
            for array in (rows, gate)
        ],
        in_specs=anywhere(2),
        out_specs=anywhere(2),
        scratch_shapes=[
            pltpu.SemaphoreType.DMA((slots,)),
            pltpu.SemaphoreType.DMA((slots,)),
            pltpu.SemaphoreType.DMA((2,)),
        ],
        compiler_params=pltpu.CompilerParams(
            collective_id=1, has_side_effects=True, vmem_limit_bytes=VMEM_BYTES
        ),
        name="spread_tokens",
    )(rows, gate)


def dot(a, b, dims=((1,), (0,))):
    return lax.dot_general(a, b, (dims, ((), ())), preferred_element_type=jnp.float32)


class PieceSum:
    def __init__(self, order, buffer, block, me, sems, count):
        self.order, self.buffer, self.block, self.me, self.sems = order, buffer, block, me, sems
        self.slots, self.index = {}, {}
        for level in range(len(order)):
            for bits in subsets(order[level + 1 :]):
                key = (level, frozenset(bits))
                self.slots[key] = len(POSITIONS) + len(self.slots)
                self.index[key] = count.next()

    def copy(self, level, bits):
        bit = self.order[level]
        key = (level, bits - {bit})
        return pltpu.make_async_remote_copy(
            src_ref=self.buffer.at[position(bits)],
            dst_ref=self.buffer.at[self.slots[key]],
            send_sem=self.sems[0].at[self.index[key]],
            recv_sem=self.sems[1].at[self.index[key]],
            device_id=moved(self.me, (bit,)),
            device_id_type=MESH,
        )

    def computed(self, bits):
        if self.order[0] in bits:
            self.copy(0, bits).start()

    def settle(self, level, bits):
        if any(bit in bits for bit in self.order[: level + 1]):
            return
        self.copy(level, bits | {self.order[level]}).wait_recv()
        kept = self.buffer.at[position(bits)]
        add_into(kept, kept, self.buffer.at[self.slots[(level, bits)]], self.block)
        if level + 1 < len(self.order) and self.order[level + 1] in bits:
            self.copy(level + 1, bits).start()

    def finish(self):
        for level, bits in self.index:
            self.copy(level, bits | {self.order[level]}).wait_send()


BLOCKS = 4


WAVES = subsets((Z_BIT, Y_BIT))
AHEAD = 1


def expert_kernel(shards, *refs):
    rows_ref, back_ref, gate_ref, in_ref, out_ref = refs[:5]
    moe_sum, grad_sum, mark_sum, half_in, half_out, grad_in, grad_out, far_in, far_out = refs[5:14]
    grad_buffers, moe_buffers, mark_buffer = refs[14:17], refs[17:20], refs[20]
    in_total, out_total, stage_in, stage_out, scaled, send, recv, local = refs[21:]
    away = [
        near + item for near in WAVES[:AHEAD] for item in subsets(far_bits(shards))[1:]
    ]
    low = jnp.bfloat16
    step = pl.program_id(0)
    block = step % BLOCKS
    me = here()
    twin = moved(me, (C_BIT,))
    sems = (send, recv)
    count = Counter()
    length = rows_ref.shape[0] // 2
    sums = [
        PieceSum(order, buffer, 128, me, sems, count)
        for turned, buffers in ((TURNED, grad_buffers), (TURNED, moe_buffers))
        for order, buffer in zip(turned, buffers)
    ]
    sums.append(PieceSum(TURNED[0], mark_buffer, length, me, sems, count))
    exchanged = [(stage_in, half_in, count.next()), (stage_out, half_out, count.next())]

    def halves():
        return [
            pltpu.make_async_remote_copy(
                src_ref=stage,
                dst_ref=half,
                send_sem=send.at[slot],
                recv_sem=recv.at[slot],
                device_id=twin,
                device_id_type=MESH,
            )
            for stage, half, slot in exchanged
        ]

    @pl.when(step == 0)
    def _():
        meet(neighbours(me, (X_BIT, C_BIT, Y_BIT, Z_BIT)) + [moved(me, bits) for bits in away])
        in_total[...] = jnp.zeros_like(in_total)
        out_total[...] = jnp.zeros_like(out_total)
        for buffer in grad_buffers + moe_buffers + (mark_buffer,):
            kept = buffer.at[pl.ds(0, len(POSITIONS))]
            kept[...] = jnp.zeros_like(kept)

    rows = rows_ref[...]
    gate = gate_ref[0]
    hidden_in = dot(rows, in_ref[0])
    gate_part = hidden_in[:, :H]
    up_part = hidden_in[:, H:]
    sigma = jax.nn.sigmoid(gate_part)
    active = gate_part * sigma
    hidden = (active * up_part).astype(low)
    width = rows.shape[1] // 3
    pair = pl.ds(2 * block, 2)

    def add_pieces(buffer, value):
        value = value.reshape((2, length) + value.shape[1:])
        buffer[pair] = (buffer[pair].astype(jnp.float32) + value).astype(low)

    mark = jnp.zeros((2 * length, 1), jnp.float32)
    for third in range(3):
        columns = slice(third * width, (third + 1) * width)
        result = dot(hidden, out_ref[0, :, columns])
        back = back_ref[:, columns].astype(jnp.float32)
        mark += jnp.sum(back * result, axis=1, keepdims=True)
        add_pieces(moe_buffers[third], gate * result)
        scaled[:, columns] = (gate * back).astype(low)
    expert = jnp.where(step < BLOCKS, twin[0], me[0]) * GROUP + me[1] % GROUP
    mark_low = mark.astype(low).astype(jnp.float32)
    lane = lax.broadcasted_iota(jnp.int32, (2 * length, 128), 1)
    add_pieces(
        mark_buffer,
        jnp.where(lane == expert, mark_low, jnp.where(lane == expert + E, mark - mark_low, 0.0)),
    )
    grad_result = scaled[...]
    grad_hidden = dot(grad_result, out_ref[0], ((1,), (1,)))
    out_total[...] += dot(hidden, grad_result, ((0,), (0,)))
    grad_gate_part = grad_hidden * up_part * sigma * (1.0 + gate_part * (1.0 - sigma))
    grad_up_part = grad_hidden * active
    grad_rows = jnp.concatenate([grad_gate_part, grad_up_part], axis=1).astype(low)
    for third in range(3):
        columns = slice(third * width, (third + 1) * width)
        add_pieces(grad_buffers[third], dot(grad_rows, in_ref[0, columns], ((1,), (1,))))
    in_total[...] += dot(rows, grad_rows, ((0,), (0,)))

    @pl.when(step == BLOCKS - 1)
    def _():
        stage_in[...] = in_total[...].astype(low)
        stage_out[...] = out_total[...].astype(low)
        for copy in halves():
            copy.start()
        in_total[...] = jnp.zeros_like(in_total)
        out_total[...] = jnp.zeros_like(out_total)

    def settle(level, number):
        for bits in POSITIONS[2 * number : 2 * number + 2]:
            for item in sums:
                item.settle(level, bits)

    for number in range(BLOCKS):

        @pl.when(step == BLOCKS + number)
        def _():
            for bits in POSITIONS[2 * number : 2 * number + 2]:
                for item in sums:
                    item.computed(bits)
            if number >= 1:
                settle(0, number - 1)
            if number >= 2:
                settle(1, number - 2)

    @pl.when(step == 2 * BLOCKS - 1)
    def _():
        loads = []
        for number, (copy, (stage, half, _)) in enumerate(zip(halves(), exchanged)):
            copy.wait()
            load = pltpu.make_async_copy(half, stage, local.at[number])
            load.start()
            loads.append(load)
        stores = []
        far_copies = []
        for number, (total, stage, goal, landed) in enumerate(
            ((in_total, stage_in, grad_in, far_in), (out_total, stage_out, grad_out, far_out))
        ):
            loads[number].wait()
            stage[...] = (total[...] + stage[...].astype(jnp.float32)).astype(low)
            store = pltpu.make_async_copy(stage, goal, local.at[2 + number])
            store.start()
            stores.append(store)
            rows_each = stage.shape[0] // shards
            for index, bits in enumerate(away):
                place = moved(me, bits)
                window = pl.ds(pl.multiple_of(place[1] * rows_each, 16), rows_each)
                far_copies.append(
                    start_copy(stage.at[window], landed.at[index], sems, count.next(), place)
                )
        settle(0, BLOCKS - 1)
        for number in (BLOCKS - 2, BLOCKS - 1):
            settle(1, number)
        for number in range(BLOCKS):
            settle(2, number)
        own = position(())
        for item, goal in zip(
            sums,
            [grad_sum.at[:, pl.ds(i * width, width)] for i in range(3)]
            + [moe_sum.at[:, pl.ds(i * width, width)] for i in range(3)]
            + [mark_sum],
        ):
            store = pltpu.make_async_copy(item.buffer.at[own], goal, local.at[len(stores) + 2])
            store.start()
            stores.append(store)
        for item in sums:
            item.finish()
        for copy in far_copies:
            copy.wait()
        for store in stores:
            store.wait()


def expert_call(rows, back, gate, full_in, full_out, shards):
    _, length, width = rows.shape
    count = len(POSITIONS) * length
    low = jnp.bfloat16
    block = 2 * length
    rows, back = rows.reshape(count, width), back.reshape(count, width)

    def weights(array):
        return pl.BlockSpec(
            (1,) + array.shape[1:], lambda i: (i // BLOCKS, 0, 0), pipeline_mode=pl.Buffered(1)
        )

    def like(array):
        return jax.ShapeDtypeStruct(array.shape[1:], low)

    sequence = jax.ShapeDtypeStruct((length, width), low)
    pieces = 2 * len(POSITIONS) - 1
    ahead = AHEAD * (shards // GROUP - 1)
    slots = 7 * 7 + 2 + 2 * ahead

    def landing(array):
        return jax.ShapeDtypeStruct((ahead, array.shape[1] // shards, array.shape[2]), low)

    return pl.pallas_call(
        functools.partial(expert_kernel, shards),
        grid=(2 * BLOCKS,),
        out_shape=[
            sequence,
            sequence,
            jax.ShapeDtypeStruct((length, 128), low),
            like(full_in),
            like(full_out),
            like(full_in),
            like(full_out),
            landing(full_in),
            landing(full_out),
        ],
        in_specs=[
            pl.BlockSpec((block, width), lambda i: (i % BLOCKS, 0)),
            pl.BlockSpec((block, width), lambda i: (i % BLOCKS, 0)),
            pl.BlockSpec((1, block, 1), lambda i: (i // BLOCKS, i % BLOCKS, 0)),
            weights(full_in),
            weights(full_out),
        ],
        out_specs=anywhere(9),
        scratch_shapes=[pltpu.VMEM((pieces, length, width // 3), low)] * 6
        + [
            pltpu.VMEM((pieces, length, 128), low),
            pltpu.VMEM(full_in.shape[1:], jnp.float32),
            pltpu.VMEM(full_out.shape[1:], jnp.float32),
            pltpu.VMEM(full_in.shape[1:], low),
            pltpu.VMEM(full_out.shape[1:], low),
            pltpu.VMEM((block, width), low),
            pltpu.SemaphoreType.DMA((slots,)),
            pltpu.SemaphoreType.DMA((slots,)),
            pltpu.SemaphoreType.DMA((12,)),
        ],
        compiler_params=pltpu.CompilerParams(
            collective_id=2,
            has_side_effects=True,
            vmem_limit_bytes=EXPERT_VMEM_BYTES,
            dimension_semantics=("arbitrary",),
        ),
        name="experts",
    )(rows, back, gate, full_in, full_out)


def turned_back(tile, tables):
    cosine, sine_up, sine_down = tables
    return (
        tile * cosine - pltpu.roll(tile, 96, 1) * sine_up - pltpu.roll(tile, 32, 1) * sine_down
    )


def close_kernel(shards, reps, *refs):
    (branch, attention, acts, lse, allowed, normed, x, grad_mid, gain, small) = refs[:10]
    tables = [ref[...] for ref in refs[10:13]]
    qkv_w, out_w, g_in, g_down, far_in, far_down = refs[13:19]
    qkv_sum, out_sum, small_sum, in_sum, down_sum, tokens_grad, qkv_part, out_part = refs[19:27]
    dense = refs[27:33]
    tiny, in_land, down_land, in_own, down_own = refs[33:38]
    qkv_held, out_held, stage, acts_grad, heads_grad, small_held = refs[38:44]
    send, recv, local = refs[44:]
    low = jnp.bfloat16
    me = here()
    sems = (send, recv)
    far = far_bits(shards)
    partners = [moved(me, item) for item in subsets((Y_BIT, Z_BIT) + far)[1:]]
    meet(neighbours(me, (X_BIT, C_BIT)) + partners)
    count, local_count = Counter(), Counter()
    sends = []
    tail = []
    loads = []
    for source, held in ((out_w, out_held), (qkv_w, qkv_held)):
        load = pltpu.make_async_copy(source, held, local.at[local_count.next()])
        load.start()
        loads.append(load)
    columns_of = []
    groups = []
    for which, (source, target) in enumerate(((qkv_part, qkv_sum), (out_part, out_sum))):
        flows = []
        rows_each = source.shape[0] // shards
        height = rows_each // len(SUM_TURNED)
        width = source.shape[1] // reps
        for number, order in enumerate(SUM_TURNED):
            buffer = dense[which * 3 + number]

            def piece(place, source=source, number=number, height=height, width=width):
                start = place[1] * (height * len(SUM_TURNED)) + number * height
                return source.at[
                    pl.ds(pl.multiple_of(start, 16), height),
                    pl.ds(pl.multiple_of(place[0] * width, 128), width),
                ]

            def goal(place, bits=(), target=target, number=number, height=height, width=width):
                return target.at[
                    pl.ds(number * height, height),
                    pl.ds(pl.multiple_of(place[0] * width, 128), width),
                ]

            flows.append(((C_BIT,) + order + far, piece, buffer, height))
            columns_of.append((buffer, goal))
        groups.append(flows)
    tiny_order = (Y_BIT, Z_BIT) + far
    rows_each = small_held.shape[0] // shards

    def tiny_piece(place):
        return small_held.at[pl.ds(pl.multiple_of(place[1] * rows_each, 16), rows_each)]

    tiny_flow = (tiny_order, tiny_piece, tiny, 16)

    def sum_run(flows):
        return sum_steps(flows, me, sems, local, count, local_count, sends)

    def last_steps():
        for buffer, goal in columns_of:
            store = pltpu.make_async_copy(buffer.at[0], goal(me), local.at[local_count.next()])
            store.start()
            tail.append(store)
        columns = [
            ((X_BIT, C_BIT), lambda place, buffer=buffer: buffer.at[0], goal, only_self)
            for buffer, goal in columns_of
        ]
        yield from gather_steps(columns, me, sems, count, sends)
        base = halving_slots(len(tiny_order))
        current = 0
        for bit in (X_BIT, C_BIT):
            slot = count.next()
            landed = tiny.at[base]
            copy = start_copy(tiny.at[current], landed, sems, slot, moved(me, (bit,)))
            copy.wait()
            add_into(tiny.at[base + 1], tiny.at[current], landed, 16)
            current = base + 1
            base += 2
            yield
        store = pltpu.make_async_copy(tiny.at[current], small_sum, local.at[local_count.next()])
        store.start()
        tail.append(store)

    arrays = (
        (g_in, far_in, in_land, in_own, in_sum),
        (g_down, far_down, down_land, down_own, down_sum),
    )
    waves = WAVES
    ahead = [near + item for near in WAVES[:AHEAD] for item in subsets(far)[1:]]

    def expert_steps():
        waiting = [[] for _ in waves]

        def send_wave(number, items):
            for item in items:
                place = moved(me, waves[number] + item)
                for source, arrived, landed, _, _ in arrays:
                    bits = waves[number] + item
                    if bits and bits not in ahead:
                        slot = count.next()
                        sends.append(
                            start_copy(source.at[place[1]], landed.at[me[1]], sems, slot, place)
                        )
                        wait = pltpu.make_async_remote_copy(
                            src_ref=landed.at[place[1]],
                            dst_ref=landed.at[place[1]],
                            send_sem=send.at[slot],
                            recv_sem=recv.at[slot],
                            device_id=place,
                            device_id_type=MESH,
                        ).wait_recv
                    else:
                        origin = arrived.at[ahead.index(bits)] if bits else source.at[me[1]]
                        load = pltpu.make_async_copy(
                            origin, landed.at[place[1]], local.at[local_count.next()]
                        )
                        load.start()
                        wait = load.wait
                    waiting[number].append(wait)

        away = subsets(far)[1:]
        for number in range(len(waves)):
            send_wave(number, ((),))
        for number in range(len(waves)):
            send_wave(number, away)
        yield
        relays = []
        for number, near in enumerate(waves):
            for wait in waiting[number]:
                wait()
            place = moved(me, near)
            expert = place[1] % GROUP
            for _, _, landed, held, target in arrays:
                total = landed.at[place[1]]
                for item in subsets(far)[1:]:
                    part = landed.at[moved(place, item)[1]]
                    add_into(held.at[number], total, part, part.shape[0])
                    total = held.at[number]

                def goal(where, bits=(), target=target, expert=expert):
                    return target.at[where[0] * GROUP + expert]

                store = pltpu.make_async_copy(total, goal(me), local.at[local_count.next()])
                store.start()
                tail.append(store)
                flow = ((X_BIT, C_BIT), lambda where, total=total: total, goal, only_self)
                relay = gather_steps([flow], me, sems, count, sends)
                relays.append(relay)
                next(relay)
            yield
        for relay in relays:
            for _ in relay:
                yield

    def weight_grad(rows, grads, part):
        width = grads.shape[1]
        stores = []
        for number in range(rows.shape[1] // 256):
            if number >= 2:
                stores[number - 2].wait()
            held = stage.at[number % 2, :, pl.ds(0, width)]
            piece = rows[:, number * 256 : (number + 1) * 256]
            held[...] = dot(piece, grads[...], ((0,), (0,))).astype(low)
            store = pltpu.make_async_copy(
                held, part.at[pl.ds(number * 256, 256)], local.at[local_count.next()]
            )
            store.start()
            stores.append(store)
        for store in stores[-2:]:
            store.wait()

    def advance(run, steps):
        for _ in range(steps):
            if next(run, "end") == "end":
                return

    experts = expert_steps()
    next(experts)
    weight_grad(attention, branch, out_part)
    out_run = sum_run(groups[1])
    next(out_run)
    loads[0].wait()
    heads_grad[...] = dot(branch[...], out_held[...], ((1,), (1,))).astype(low)

    lane = lax.broadcasted_iota(jnp.int32, (1, 128), 1)
    sides = [(lane < HD).astype(jnp.float32), (lane >= HD).astype(jnp.float32)]
    sides_low = [side.astype(low) for side in sides]
    scale = HD ** (-0.5)
    group = HEADS // KV_HEADS

    def doubled(tile):
        tile = tile.astype(jnp.float32)
        other = pltpu.roll(tile, HD, 1)
        return [
            (tile * sides[0] + other * sides[1]).astype(low),
            (other * sides[0] + tile * sides[1]).astype(low),
        ]

    for pair in range(KV_HEADS // 2):
        keys = doubled(acts[:, QD + 128 * pair : QD + 128 * (pair + 1)])
        values = doubled(acts[:, QD + KVD + 128 * pair : QD + KVD + 128 * (pair + 1)])
        query_grads = [None] * group
        key_tile = value_tile = None
        for half in range(2):
            key_total = value_total = None
            for number in range(group):
                head = (2 * pair + half) * group + number
                tile, side = head // 2, head % 2
                columns = slice(128 * tile, 128 * (tile + 1))
                query = acts[:, columns] * sides_low[side]
                grad_out = heads_grad[:, columns] * sides_low[side]
                scores = dot(query, keys[half], ((1,), (1,))) * scale
                scores = jnp.where(allowed[...] > 0.5, scores, masked_score)
                probs = jnp.exp(scores - lse[:, head : head + 1])
                grad_probs = dot(grad_out, values[half], ((1,), (1,)))
                inner = jnp.sum(grad_probs * probs, axis=1, keepdims=True)
                grad_scores = (probs * (grad_probs - inner)).astype(low)
                value_part = dot(probs.astype(low), grad_out, ((0,), (0,)))
                key_part = dot(grad_scores, query, ((0,), (0,)))
                query_part = dot(grad_scores, keys[half]) * sides[side]
                local_tile = tile - group * pair
                if query_grads[local_tile] is None:
                    query_grads[local_tile] = query_part
                else:
                    query_grads[local_tile] += query_part
                key_total = key_part if key_total is None else key_total + key_part
                value_total = value_part if value_total is None else value_total + value_part
            key_total = (key_total + pltpu.roll(key_total, HD, 1)) * sides[half]
            value_total = (value_total + pltpu.roll(value_total, HD, 1)) * sides[half]
            key_tile = key_total if key_tile is None else key_tile + key_total
            value_tile = value_total if value_tile is None else value_tile + value_total
        for number in range(group):
            tile = group * pair + number
            acts_grad[:, 128 * tile : 128 * (tile + 1)] = turned_back(
                query_grads[number] * scale, tables
            ).astype(low)
        acts_grad[:, QD + 128 * pair : QD + 128 * (pair + 1)] = turned_back(
            key_tile * scale, tables
        ).astype(low)
        acts_grad[:, QD + KVD + 128 * pair : QD + KVD + 128 * (pair + 1)] = value_tile.astype(low)
        advance(out_run, OUT_STEPS[pair])
        advance(experts, EARLY[pair])

    weight_grad(normed, acts_grad, qkv_part)
    qkv_run = sum_run(groups[0])
    next(qkv_run)
    loads[1].wait()
    grad_normed = dot(acts_grad[...], qkv_held[...], ((1,), (1,)))
    value = x[...].astype(jnp.float32)
    spread = lax.rsqrt(jnp.mean(value * value, axis=-1, keepdims=True) + norm_eps)
    normal = value * spread
    inner = grad_normed * gain[...]
    tokens_grad[...] = grad_mid[...] + spread * (
        inner - normal * jnp.mean(inner * normal, axis=-1, keepdims=True)
    )
    gain_grad = lax.dot_general(
        grad_normed * normal,
        jnp.ones((value.shape[0], 128), jnp.float32),
        (((0,), (0,)), ((), ())),
        precision=HIGH,
        preferred_element_type=jnp.float32,
    )
    column = lax.broadcasted_iota(jnp.int32, gain_grad.shape, 1)
    small_held[...] = jnp.where(
        column == E, gain_grad, small[...].astype(jnp.float32)
    ).astype(low)
    third = sum_run([tiny_flow])
    next(third)

    mixed = [(qkv_run, 6), (out_run, 6), (experts, 1), (third, 1)]
    alive = [run for run, _ in mixed]
    while alive:
        for run, turns in mixed:
            for _ in range(turns):
                if run in alive and next(run, "end") == "end":
                    alive.remove(run)
    for _ in last_steps():
        pass
    for copy in sends:
        copy.wait_send()
    for copy in tail:
        copy.wait()


def close_call(near, weights, experts, shards, reps):
    branch, acts, small = near[0], near[2], near[9]
    qkv_w, out_w = weights
    g_in, g_down = experts[:2]
    far = far_bits(shards)
    size = 4 + len(far)
    pieces = halving_slots(size)
    low = jnp.bfloat16
    length = branch.shape[0]

    def part(array):
        return array.shape[0] // shards, array.shape[1]

    def dense_buffer(array):
        rows, columns = part(array)
        return [pltpu.VMEM((pieces, rows // 3, columns // reps), low)] * 3

    small_rows = small.shape[0] // shards
    tiny_pieces = halving_slots(2 + len(far)) + 4
    slots = 7 * (2**size - 1) + 2 * shards + 14 * 3 + 4
    vmem = pl.BlockSpec(memory_space=pltpu.VMEM)
    return pl.pallas_call(
        functools.partial(close_kernel, shards, reps),
        out_shape=[
            jax.ShapeDtypeStruct(part(qkv_w), low),
            jax.ShapeDtypeStruct(part(out_w), low),
            jax.ShapeDtypeStruct((small_rows, 128), low),
        ]
        + [
            jax.ShapeDtypeStruct((reps * GROUP,) + array.shape[1:], low) for array in (g_in, g_down)
        ]
        + [
            jax.ShapeDtypeStruct((length, D), jnp.float32),
            jax.ShapeDtypeStruct(qkv_w.shape, low),
            jax.ShapeDtypeStruct(out_w.shape, low),
        ],
        in_specs=[vmem] * len(near) + anywhere(6),
        out_specs=anywhere(5) + [vmem] + anywhere(2),
        scratch_shapes=dense_buffer(qkv_w)
        + dense_buffer(out_w)
        + [
            pltpu.VMEM((tiny_pieces, small_rows, 128), low),
            pltpu.VMEM(g_in.shape, low),
            pltpu.VMEM(g_down.shape, low),
            pltpu.VMEM((GROUP,) + g_in.shape[1:], low),
            pltpu.VMEM((GROUP,) + g_down.shape[1:], low),
            pltpu.VMEM(qkv_w.shape, low),
            pltpu.VMEM(out_w.shape, low),
            pltpu.VMEM((2, 256, qkv_w.shape[1]), low),
            pltpu.VMEM(acts.shape, low),
            pltpu.VMEM(branch.shape, low),
            pltpu.VMEM(small.shape, low),
            pltpu.SemaphoreType.DMA((slots,)),
            pltpu.SemaphoreType.DMA((slots,)),
            pltpu.SemaphoreType.DMA((7 * 2 ** (size - 1) + 64,)),
        ],
        compiler_params=pltpu.CompilerParams(
            collective_id=3, has_side_effects=True, vmem_limit_bytes=EXPERT_VMEM_BYTES
        ),
        name="close_sums",
    )(*near, *weights, *experts)


def on_device(
    shards,
    reps,
    tokens,
    segments,
    routes,
    cotangent,
    wqkv,
    wqkv_first,
    wqkv_second,
    wo,
    wo_first,
    wo_second,
    router,
    router_first,
    router_second,
    w_in,
    w_in_first,
    w_in_second,
    w_out,
    w_out_first,
    w_out_second,
    gains,
    gains_first,
    gains_second,
):
    length, width = tokens.shape
    group = HEADS // KV_HEADS
    segs = segments[0]
    rep, shard = here()
    low = jnp.bfloat16

    def cut(array):
        return array.astype(low).reshape((shards, array.shape[0] // shards) + array.shape[1:])

    small = jnp.concatenate(
        [router, gains.T, jnp.zeros((router.shape[0], 128 - E - 2), jnp.float32)], axis=1
    ).astype(low)
    mine_in = lax.dynamic_slice_in_dim(w_in, rep * GROUP, GROUP, 0).astype(low)
    mine_out = lax.dynamic_slice_in_dim(w_out, rep * GROUP, GROUP, 0).astype(low)
    qkv_w, out_w, small_w, full_in, full_out, cot_all = open_call(
        wqkv.astype(low), wo.astype(low), small, mine_in, mine_out, cotangent, shards, reps
    )
    qkv_w = qkv_w.reshape(D, -1)
    out_w = out_w.reshape(QD, D)
    small_w = small_w.reshape(D, 128)
    router_w = small_w[:, :E]
    gain_f = small_w[:, E : E + 2].astype(jnp.float32).T

    x = tokens.astype(jnp.float32)
    normed = rms_norm(x, gain_f[0]).astype(low)
    qkv = jnp.dot(normed, qkv_w, preferred_element_type=jnp.float32)
    query = (
        rotary(qkv[:, :QD].reshape(length, HEADS, HD))
        .astype(low)
        .reshape(length, KV_HEADS, group, HD)
    )
    keys = rotary(qkv[:, QD : QD + KVD].reshape(length, KV_HEADS, HD)).astype(low)
    values = qkv[:, QD + KVD :].reshape(length, KV_HEADS, HD).astype(low)
    attended, lses = attend_forward(query, keys, values, segs)
    attention = attended.reshape(length, QD)
    branch = jnp.dot(attention, out_w, preferred_element_type=jnp.float32)
    mid = x + branch
    normed2 = rms_norm(mid, gain_f[1]).astype(low)
    logits = jnp.dot(normed2, router_w, preferred_element_type=jnp.float32)
    picks = (routes[:, :, None] == jnp.arange(E, dtype=jnp.int32)[None, None, :]).any(axis=1)
    gates = jax.nn.softmax(jnp.where(picks, logits, -jnp.inf), axis=-1)

    rows, gates_all = spread_call(normed2, gates.T)
    gate = jnp.stack(
        [
            lax.dynamic_index_in_dim(gates_all, flip(rep, 0) * GROUP + shard % GROUP, 1, False),
            lax.dynamic_index_in_dim(gates_all, rep * GROUP + shard % GROUP, 1, False),
        ]
    ).reshape(2, -1, 1)
    moe, grad_normed2, marks, _, _, grad_in, grad_down, far_in, far_down = expert_call(
        rows, cot_all, gate, full_in.reshape(2, D, 2 * H), full_out.reshape(2, H, D), shards
    )
    marks = marks.astype(jnp.float32)
    grad_gates = marks[:, :E] + marks[:, E : 2 * E]
    mixed = (mid + moe.astype(jnp.float32)).astype(low)

    grad_logits = gates * (grad_gates - jnp.sum(grad_gates * gates, axis=-1, keepdims=True))
    grad_router = jnp.dot(normed2.astype(jnp.float32).T, grad_logits, precision=HIGH)
    grad_normed2 = grad_normed2.astype(jnp.float32) + jnp.dot(
        grad_logits, router_w.astype(jnp.float32).T, precision=HIGH
    )
    cot = cotangent.astype(jnp.float32)
    grad_mid_norm, grad_gain2 = norm_back(mid, gain_f[1], grad_normed2)
    grad_mid = cot + grad_mid_norm
    grad_branch = grad_mid.astype(low)
    grad_small = jnp.concatenate(
        [
            grad_router,
            jnp.zeros((D, 1), jnp.float32),
            grad_gain2[:, None],
            jnp.zeros((D, 128 - E - 2), jnp.float32),
        ],
        axis=1,
    ).astype(low)
    acts = jnp.concatenate(
        [query.reshape(length, QD), keys.reshape(length, KVD), values.reshape(length, KVD)], axis=1
    )
    lse_columns = jnp.pad(lses.reshape(HEADS, length).T, ((0, 0), (0, 128 - HEADS)))
    places = jnp.arange(length, dtype=jnp.int32)
    allowed = (places[:, None] >= places[None, :]) & (segs[:, None] == segs[None, :])
    cosine, sine, _ = angle_tables(length, HD)
    cosine, sine = cosine[:, 0], sine[:, 0]
    blank = jnp.zeros_like(sine)
    grad_qkv_w, grad_out_w, grad_small, grad_in_all, grad_down_all, tokens_grad, _, _ = close_call(
        (
            grad_branch,
            attention,
            acts,
            lse_columns,
            allowed.astype(jnp.float32),
            normed,
            tokens,
            grad_mid,
            gain_f[:1],
            grad_small,
            jnp.concatenate([cosine] * 4, axis=1),
            jnp.concatenate([-sine, blank] * 2, axis=1),
            jnp.concatenate([blank, sine] * 2, axis=1),
        ),
        (qkv_w, out_w),
        (cut(grad_in), cut(grad_down), far_in, far_down),
        shards,
        reps,
    )
    grad_small = grad_small.astype(jnp.float32)
    grad_router = grad_small[:, :E]
    grad_gains = grad_small[:, E : E + 2].T
    qkv_m, qkv_v, qkv_new = adamw(
        wqkv, wqkv_first, wqkv_second, grad_qkv_w.astype(jnp.float32), 3.0 * D ** (-0.5), decay_rate
    )
    out_m, out_v, out_new = adamw(
        wo, wo_first, wo_second, grad_out_w.astype(jnp.float32), 3.0 * (QD // 64) ** (-0.5), decay_rate
    )
    rout_m, rout_v, rout_new = adamw(
        router, router_first, router_second, grad_router, 1.5 * D ** (-0.5), decay_rate
    )
    in_m, in_v, in_new = adamw(
        w_in, w_in_first, w_in_second, grad_in_all.astype(jnp.float32), 3.0 * D ** (-0.5), decay_rate
    )
    down_m, down_v, down_new = adamw(
        w_out,
        w_out_first,
        w_out_second,
        grad_down_all.astype(jnp.float32),
        3.0 * (H // 16) ** (-0.5),
        decay_rate,
    )
    gain_m, gain_v, gain_new = adamw(gains, gains_first, gains_second, grad_gains, 0.6, 0.0)
    return (
        mixed,
        tokens_grad,
        qkv_m,
        qkv_v,
        qkv_new,
        out_m,
        out_v,
        out_new,
        rout_m,
        rout_v,
        rout_new,
        in_m,
        in_v,
        in_new,
        down_m,
        down_v,
        down_new,
        gain_m,
        gain_v,
        gain_new,
    )


def solution(mesh):
    in_specs = (
        P(("rep", "shard"), None),
        P(("rep", "shard"), None),
        P(("rep", "shard"), None),
        P(("rep", "shard"), None),
        P("shard", None),
        P("shard", None),
        P("shard", None),
        P("shard", None),
        P("shard", None),
        P("shard", None),
        P("shard", None),
        P("shard", None),
        P("shard", None),
        P(None, "shard", None),
        P(None, "shard", None),
        P(None, "shard", None),
        P(None, "shard", None),
        P(None, "shard", None),
        P(None, "shard", None),
        P(None, "shard"),
        P(None, "shard"),
        P(None, "shard"),
    )
    out_specs = (
        P(("rep", "shard"), None),
        P(("rep", "shard"), None),
        P("shard", None),
        P("shard", None),
        P("shard", None),
        P("shard", None),
        P("shard", None),
        P("shard", None),
        P("shard", None),
        P("shard", None),
        P("shard", None),
        P(None, "shard", None),
        P(None, "shard", None),
        P(None, "shard", None),
        P(None, "shard", None),
        P(None, "shard", None),
        P(None, "shard", None),
        P(None, "shard"),
        P(None, "shard"),
        P(None, "shard"),
    )
    return jax.shard_map(
        functools.partial(on_device, mesh.shape["shard"], mesh.shape["rep"]), mesh=mesh, in_specs=in_specs, out_specs=out_specs, check_vma=False
    )
```

profile of v0, /device:TPU:0, one launch (start us, length us, event | category | flops | bytes accessed | tf_op | source)
XLA Modules:
  0.0 640.2 jit_solution(12975014689506197345)
XLA Ops:
  0.7 3.4 dynamic-slice_convert_fusion.refs_3_
  4.1 2.4 dynamic-slice_convert_fusion.1.refs_4_
  10.1 148.9 %open_gather.1 = (bf16[8,192,2560]{2,1,0:T(8,128)(2,1)}, bf16[8,192,1536]{2,1,0:T(8,128)(2,1)}, bf16[8,192,128]{2,1,0:T(8,128)(2,1)}, bf16[2,8,192,1024]{3,2,1,0...) custom-call(bf16[192,2560]{1,0:T(8,128)(2,1)} %convert_element_type.96.refs_0_, ...), custom_call_target="tpu_custom_call" | custom-call | tf_op jit(solution)/shard_map/open_gather/pallas_call | solution.py:564
  161.7 5.7 fusion.51
  167.5 1.5 copy-done.11
  168.9 1.2 slice.68
  170.2 1.9 copy.233
  177.8 1.4 exponential_reduce_fusion
  179.2 1.7 copy-done.6
  181.7 4.9 fusion.15
  186.7 1.5 multiply_reduce_fusion.2
  190.7 49.0 %spread_tokens.1 = (bf16[8,256,1536]{2,1,0:T(8,128)(2,1)}, f32[8,16,256]{2,1,0:T(8,128)}) custom-call(bf16[256,1536]{1,0:T(8,128)(2,1)} %copy-done.3, f32[16,256]{1,0:T(8,128)} %copy.239.refs_1_), custom_call_target="tpu_custom_call" | custom-call | tf_op jit(solution)/shard_map/spread_tokens/pallas_call | solution.py:610
  241.0 1.4 copy.241
  242.4 2.7 pad_maximum_fusion.refs_2_
  245.0 147.9 %experts.1 = (bf16[256,1536]{1,0:T(8,128)(2,1)}, bf16[256,1536]{1,0:T(8,128)(2,1)}, bf16[256,128]{1,0:T(8,128)(2,1)}, bf16[1536,1024]{1,0:T(8,128)(2,1)}, bf16[5...) custom-call(bf16[2048,1536]{1,0:T(8,128)(2,1)} %bitcast.78, ...), custom_call_target="tpu_custom_call" | custom-call | tf_op jit(solution)/shard_map/experts/pallas_call | solution.py:865
  395.7 1.6 convolution_convert_fusion
  397.6 3.5 multiply_reduce_fusion
  403.9 2.3 pad_maximum_fusion.1.refs_2_
  406.2 4.1 fusion.49
  413.4 168.3 %close_sums.1 = (bf16[192,2560]{1,0:T(8,128)(2,1)}, bf16[192,1536]{1,0:T(8,128)(2,1)}, bf16[192,128]{1,0:T(8,128)(2,1)}, bf16[16,192,1024]{2,1,0:T(8,128)(2,1)},...) custom-call(bf16[256,1536]{1,0:T(8,128)(2,1)} %get-tuple-element.206, ...), custom_call_target="tpu_custom_call" | custom-call | tf_op jit(solution)/shard_map/close_sums/pallas_call | solution.py:1223
  584.1 30.6 %multiply_subtract_fusion = (f32[16,192,1024]{2,1,0:T(8,128)}, f32[16,192,1024]{2,1,0:T(8,128)}, f32[16,192,1024]{2,1,0:T(8,128)}) fusion(f32[16,192,1024]{2,1,0:T(8,128)} %param.35, bf16[16,192,1024]{2,1,0:T(8,128)(2,1)} %get-tuple-element.81, f32[16,192,1024]{2,1,0:T(8,128)} %param.37, f32[16,192,1024]{2,1,0:T(8,128)} %param.36), kind=kLoop, calls=%fused_computation.4 | loop fusion | flops 50331648 | bytes 81788928 | tf_op jit(solution)/shard_map/sub | solution.py:380
  614.7 14.0 %multiply_subtract_fusion.1 = (f32[16,64,1536]{2,1,0:T(8,128)}, f32[16,64,1536]{2,1,0:T(8,128)}, f32[16,64,1536]{2,1,0:T(8,128)}) fusion(f32[16,64,1536]{2,1,0:T(8,128)} %param.38, bf16[16,64,1536]{2,1,0:T(8,128)(2,1)S(1)} %copy-done.10, f32[16,64,1536]{2,1,0:T(8,128)} %param.40, f32[16,64,1536]{2,1,0:T(8,128)} %param.39), kind=kLoop, calls=%fused_computation.10 | loop fusion | flops 25165824 | bytes 40894464 | tf_op jit(solution)/shard_map/sub | solution.py:380
  628.8 3.6 multiply_subtract_fusion.2
  632.5 2.4 multiply_subtract_fusion.3
  (185 shorter events, 32.6 us)
Async XLA Ops:
  0.7 5.8 copy-start.35
  0.7 6.6 %copy-start.37 = (f32[2,192]{1,0:T(2,128)S(1)}, f32[2,192]{1,0:T(2,128)}, u32[]{:S(2)}) copy-start(f32[2,192]{1,0:T(2,128)} %param.41) | copy-start | bytes 4612
  0.7 7.5 %copy-start.1 = (f32[192,2560]{1,0:T(8,128)S(1)}, f32[192,2560]{1,0:T(8,128)}, u32[]{:S(2)}) copy-start(f32[192,2560]{1,0:T(8,128)} %param.26) | copy-start | bytes 5898244
  161.7 5.8 copy-start.9
  177.8 3.7 copy-start.12
  181.6 5.1 slice-start
  181.7 5.0 slice-start.1
  189.8 50.8 %copy-start.38 = (f32[256]{0:T(256)}, f32[256]{0:T(256)S(1)}, u32[]{:S(2)}) copy-start(f32[256]{0:T(256)S(1)} %fusion.30) | copy-start | bytes 3076
  393.0 4.6 copy-start.17
  393.0 4.6 copy-start.40
  397.6 3.9 copy-start.46
  397.6 4.9 copy-start.19
  397.6 4.9 copy-start.21
  406.2 4.1 copy-start.5
  413.4 169.2 %copy-start.47 = (f32[2,192]{1,0:T(2,128)S(1)}, f32[2,192]{1,0:T(2,128)}, u32[]{:S(2)}) copy-start(f32[2,192]{1,0:T(2,128)} %param.42) | copy-start | bytes 4612
  413.4 169.3 %copy-start.48 = (f32[2,192]{1,0:T(2,128)S(1)}, f32[2,192]{1,0:T(2,128)}, u32[]{:S(2)}) copy-start(f32[2,192]{1,0:T(2,128)} %param.43) | copy-start | bytes 4612
  584.1 30.6 %copy-start.10 = (bf16[16,64,1536]{2,1,0:T(8,128)(2,1)S(1)}, bf16[16,64,1536]{2,1,0:T(8,128)(2,1)}, u32[]{:S(2)}) copy-start(bf16[16,64,1536]{2,1,0:T(8,128)(2,1)} %get-tuple-element.82) | copy-start | bytes 9437188
  614.7 14.1 %copy-start.2 = (f32[192,2560]{1,0:T(8,128)S(1)}, f32[192,2560]{1,0:T(8,128)}, u32[]{:S(2)}) copy-start(f32[192,2560]{1,0:T(8,128)} %param.26) | copy-start | bytes 5898244
  614.7 14.1 %copy-start.13 = (f32[192,2560]{1,0:T(8,128)S(1)}, f32[192,2560]{1,0:T(8,128)}, u32[]{:S(2)}) copy-start(f32[192,2560]{1,0:T(8,128)} %param.28) | copy-start | bytes 5898244
  614.7 14.1 %copy-start.14 = (f32[192,2560]{1,0:T(8,128)S(1)}, f32[192,2560]{1,0:T(8,128)}, u32[]{:S(2)}) copy-start(f32[192,2560]{1,0:T(8,128)} %param.27) | copy-start | bytes 5898244
  614.7 14.1 %copy-start.28 = (bf16[192,2560]{1,0:T(8,128)(2,1)S(1)}, bf16[192,2560]{1,0:T(8,128)(2,1)}, u32[]{:S(2)}) copy-start(bf16[192,2560]{1,0:T(8,128)(2,1)} %get-tuple-element.78) | copy-start | bytes 2949124
  628.8 3.7 copy-start.8
  628.8 3.7 copy-start.26
  635.0 3.9 copy-start.15
  (28 other events, 56.6 us)
where the time goes:
time: 649 us; the launch traced here: 640 us
  Pallas kernels  514 us (79%)
  other arithmetic  75.7 us (12%)
  local copies, waits for them, and re-layouts  29.9 us (5%)
  matrix products  18.7 us (3%)
    pallas_call x1, Pallas kernels, close_call(): pl.pallas_call(functools.partial(close_kernel, shards, reps), out_shape=[...  168 us
    pallas_call x1, Pallas kernels, open_call(): pl.pallas_call(functools.partial(open_kernel, shards, reps), out_shape=sh...  149 us
    pallas_call x1, Pallas kernels, expert_call(): pl.pallas_call(functools.partial(expert_kernel, shards), grid=(2 * BLOCKS...  148 us
    sub x6, other arithmetic, adamw(): return (first_new, second_new, weight - rate * (update + decay * weight))  50.8 us
    pallas_call x1, Pallas kernels, spread_call(): pl.pallas_call(spread_kernel, out_shape=[jax.ShapeDtypeStruct((len(POSITI...  49 us

commit v1 on v0

--- a/solution.py
+++ b/solution.py
@@ -28,8 +28,9 @@
 decay_rate = 0.1
 masked_score = -1e30
 HOOK = 0
-OUT_STEPS = (0, 24, 24, 24)
-EARLY = (1, 1, 1, 1)
+OUT_STEPS = (0, 3, 0, 0)
+PIECE = 384
+EARLY = (1, 1, 0, 1)
 VMEM_BYTES = 56 * 2**20
 EXPERT_VMEM_BYTES = 62 * 2**20
 
@@ -631,6 +632,85 @@
     return lax.dot_general(a, b, (dims, ((), ())), preferred_element_type=jnp.float32)
 
 
+def bit_of(place, bit):
+    return (place[0 if bit[0] == "r" else 1] // 2 ** bit[1]) % 2
+
+
+class BlockSum:
+    def __init__(self, order, source, rows, width, kept, lands, tools):
+        self.order, self.source, self.rows, self.width = order, source, rows, width
+        self.kept, self.lands = kept, lands
+        self.me, self.sems, self.local, self.count, self.local_count, self.sends = tools
+        self.mine = {bit: bit_of(self.me, bit) for bit in order}
+        shard_bits = sorted((bit for bit in order if bit[0] == "s"), reverse=True)
+        self.dims = (X_BIT,) + tuple(shard_bits)
+        self.waits = {}
+
+    def at(self, ref, level, chosen):
+        left = [bit for bit in self.dims if bit not in self.order[1 : level + 1]]
+        return ref.at[tuple(chosen.get(bit, slice(None)) for bit in left)]
+
+    def begin(self):
+        waits = []
+        twin = moved(self.me, (C_BIT,))
+        for x in range(2):
+
+            def columns(c):
+                start = pl.multiple_of((2 * x + c) * self.width, 128)
+                window = (slice(None),) * (len(self.dims) - 1)
+                return self.source.at[window + (self.rows, pl.ds(start, self.width))]
+
+            core = self.mine[C_BIT]
+            landed = self.lands[0].at[x]
+            copy = start_copy(columns(1 - core), landed, self.sems, self.count.next(), twin)
+            self.sends.append(copy)
+            load = pltpu.make_async_copy(
+                columns(core), self.kept.at[x], self.local.at[self.local_count.next()]
+            )
+            load.start()
+            waits += [copy.wait_recv, load.wait]
+        self.waits[0] = waits
+
+    def step(self, level):
+        for wait in self.waits[level]:
+            wait()
+        fixed = {bit: self.mine[bit] for bit in self.order[1 : level + 1]}
+        following = self.order[level + 1] if level + 1 < len(self.order) else None
+        rest = [bit for bit in self.dims if bit not in fixed and bit != following]
+        sides = (1 - self.mine[following], self.mine[following]) if following else (None,)
+        for number, side in enumerate(sides):
+            for mask in range(2 ** len(rest)):
+                chosen = {bit: (mask >> i) % 2 for i, bit in enumerate(rest)}
+                if following:
+                    chosen[following] = side
+                landed = self.at(self.lands[level], level, chosen)
+                kept = self.at(self.kept, 0, {**fixed, **chosen})
+                add_into(kept, kept, landed, kept.shape[0])
+            if following and number == 0:
+                copy = start_copy(
+                    self.at(self.kept, 0, {**fixed, following: side}),
+                    self.lands[level + 1],
+                    self.sems,
+                    self.count.next(),
+                    moved(self.me, (following,)),
+                )
+                self.sends.append(copy)
+                self.waits[level + 1] = [copy.wait_recv]
+
+    def result(self):
+        return self.at(self.kept, 0, {bit: self.mine[bit] for bit in self.dims})
+
+
+def block_steps(sums):
+    for item in sums:
+        item.begin()
+    yield
+    for level in range(len(sums[0].order)):
+        for item in sums:
+            item.step(level)
+            yield
+
+
 class PieceSum:
     def __init__(self, order, buffer, block, me, sems, count):
         self.order, self.buffer, self.block, self.me, self.sems = order, buffer, block, me, sems
@@ -918,10 +998,12 @@
     tables = [ref[...] for ref in refs[10:13]]
     qkv_w, out_w, g_in, g_down, far_in, far_down = refs[13:19]
     qkv_sum, out_sum, small_sum, in_sum, down_sum, tokens_grad, qkv_part, out_part = refs[19:27]
-    dense = refs[27:33]
-    tiny, in_land, down_land, in_own, down_own = refs[33:38]
-    qkv_held, out_held, stage, acts_grad, heads_grad, small_held = refs[38:44]
-    send, recv, local = refs[44:]
+    levels = 4 + len(far_bits(shards))
+    dense = refs[27 : 27 + 6 * (levels + 1)]
+    refs = refs[27 + 6 * (levels + 1) :]
+    tiny, in_land, down_land, in_own, down_own = refs[:5]
+    qkv_held, out_held, stage, acts_grad, heads_grad, small_held = refs[5:11]
+    send, recv, local = refs[11:]
     low = jnp.bfloat16
     me = here()
     sems = (send, recv)
@@ -938,30 +1020,24 @@
         loads.append(load)
     columns_of = []
     groups = []
+    tools = (me, sems, local, count, local_count, sends)
     for which, (source, target) in enumerate(((qkv_part, qkv_sum), (out_part, out_sum))):
-        flows = []
-        rows_each = source.shape[0] // shards
-        height = rows_each // len(SUM_TURNED)
-        width = source.shape[1] // reps
+        group = []
+        height = source.shape[-2] // len(SUM_TURNED)
+        width = source.shape[-1] // reps
         for number, order in enumerate(SUM_TURNED):
-            buffer = dense[which * 3 + number]
-
-            def piece(place, source=source, number=number, height=height, width=width):
-                start = place[1] * (height * len(SUM_TURNED)) + number * height
-                return source.at[
-                    pl.ds(pl.multiple_of(start, 16), height),
-                    pl.ds(pl.multiple_of(place[0] * width, 128), width),
-                ]
-
-            def goal(place, bits=(), target=target, number=number, height=height, width=width):
-                return target.at[
-                    pl.ds(number * height, height),
-                    pl.ds(pl.multiple_of(place[0] * width, 128), width),
-                ]
-
-            flows.append(((C_BIT,) + order + far, piece, buffer, height))
-            columns_of.append((buffer, goal))
-        groups.append(flows)
+            buffers = dense[(3 * which + number) * (levels + 1) :][: levels + 1]
+            rows = pl.ds(number * height, height)
+            total = BlockSum(
+                (C_BIT,) + order + far, source, rows, width, buffers[0], buffers[1:], tools
+            )
+
+            def goal(place, bits=(), target=target, rows=rows, width=width):
+                return target.at[rows, pl.ds(pl.multiple_of(place[0] * width, 128), width)]
+
+            group.append(total)
+            columns_of.append((total, goal))
+        groups.append(group)
     tiny_order = (Y_BIT, Z_BIT) + far
     rows_each = small_held.shape[0] // shards
 
@@ -974,13 +1050,13 @@
         return sum_steps(flows, me, sems, local, count, local_count, sends)
 
     def last_steps():
-        for buffer, goal in columns_of:
-            store = pltpu.make_async_copy(buffer.at[0], goal(me), local.at[local_count.next()])
+        for total, goal in columns_of:
+            store = pltpu.make_async_copy(total.result(), goal(me), local.at[local_count.next()])
             store.start()
             tail.append(store)
         columns = [
-            ((X_BIT, C_BIT), lambda place, buffer=buffer: buffer.at[0], goal, only_self)
-            for buffer, goal in columns_of
+            ((X_BIT, C_BIT), lambda place, total=total: total.result(), goal, only_self)
+            for total, goal in columns_of
         ]
         yield from gather_steps(columns, me, sems, count, sends)
         base = halving_slots(len(tiny_order))
@@ -1071,19 +1147,28 @@
 
     def weight_grad(rows, grads, part):
         width = grads.shape[1]
+        rows_each = part.shape[-2]
+        shard_bits = part.ndim - 2
         stores = []
-        for number in range(rows.shape[1] // 256):
+        for number in range(rows.shape[1] // PIECE):
             if number >= 2:
-                stores[number - 2].wait()
+                for store in stores[number - 2]:
+                    store.wait()
             held = stage.at[number % 2, :, pl.ds(0, width)]
-            piece = rows[:, number * 256 : (number + 1) * 256]
+            piece = rows[:, number * PIECE : (number + 1) * PIECE]
             held[...] = dot(piece, grads[...], ((0,), (0,))).astype(low)
-            store = pltpu.make_async_copy(
-                held, part.at[pl.ds(number * 256, 256)], local.at[local_count.next()]
-            )
-            store.start()
-            stores.append(store)
-        for store in stores[-2:]:
+            stores.append([])
+            for inner in range(PIECE // rows_each):
+                index = number * (PIECE // rows_each) + inner
+                spot = tuple((index >> bit) % 2 for bit in reversed(range(shard_bits)))
+                store = pltpu.make_async_copy(
+                    held.at[pl.ds(inner * rows_each, rows_each)],
+                    part.at[spot],
+                    local.at[local_count.next()],
+                )
+                store.start()
+                stores[-1].append(store)
+        for store in stores[-2] + stores[-1]:
             store.wait()
 
     def advance(run, steps):
@@ -1094,7 +1179,7 @@
     experts = expert_steps()
     next(experts)
     weight_grad(attention, branch, out_part)
-    out_run = sum_run(groups[1])
+    out_run = block_steps(groups[1])
     next(out_run)
     loads[0].wait()
     heads_grad[...] = dot(branch[...], out_held[...], ((1,), (1,))).astype(low)
@@ -1159,7 +1244,7 @@
         advance(experts, EARLY[pair])
 
     weight_grad(normed, acts_grad, qkv_part)
-    qkv_run = sum_run(groups[0])
+    qkv_run = block_steps(groups[0])
     next(qkv_run)
     loads[1].wait()
     grad_normed = dot(acts_grad[...], qkv_held[...], ((1,), (1,)))
@@ -1184,7 +1269,7 @@
     third = sum_run([tiny_flow])
     next(third)
 
-    mixed = [(qkv_run, 6), (out_run, 6), (experts, 1), (third, 1)]
+    mixed = [(qkv_run, 1), (out_run, 1), (experts, 1), (third, 1)]
     alive = [run for run, _ in mixed]
     while alive:
         for run, turns in mixed:
@@ -1205,7 +1290,6 @@
     g_in, g_down = experts[:2]
     far = far_bits(shards)
     size = 4 + len(far)
-    pieces = halving_slots(size)
     low = jnp.bfloat16
     length = branch.shape[0]
 
@@ -1214,7 +1298,11 @@
 
     def dense_buffer(array):
         rows, columns = part(array)
-        return [pltpu.VMEM((pieces, rows // 3, columns // reps), low)] * 3
+        shapes = [(2,) * (size - 1)] + [(2,) * (size - 1 - level) for level in range(size)]
+        return [pltpu.VMEM(shape + (rows // 3, columns // reps), low) for shape in shapes] * 3
+
+    def by_bits(array):
+        return jax.ShapeDtypeStruct((2,) * (size - 2) + part(array), low)
 
     small_rows = small.shape[0] // shards
     tiny_pieces = halving_slots(2 + len(far)) + 4
@@ -1232,8 +1320,8 @@
         ]
         + [
             jax.ShapeDtypeStruct((length, D), jnp.float32),
-            jax.ShapeDtypeStruct(qkv_w.shape, low),
-            jax.ShapeDtypeStruct(out_w.shape, low),
+            by_bits(qkv_w),
+            by_bits(out_w),
         ],
         in_specs=[vmem] * len(near) + anywhere(6),
         out_specs=anywhere(5) + [vmem] + anywhere(2),
@@ -1247,7 +1335,7 @@
             pltpu.VMEM((GROUP,) + g_down.shape[1:], low),
             pltpu.VMEM(qkv_w.shape, low),
             pltpu.VMEM(out_w.shape, low),
-            pltpu.VMEM((2, 256, qkv_w.shape[1]), low),
+            pltpu.VMEM((2, PIECE, qkv_w.shape[1]), low),
             pltpu.VMEM(acts.shape, low),
             pltpu.VMEM(branch.shape, low),
             pltpu.VMEM(small.shape, low),

time: 649 us -> 647 us (level)
  no operation moved by 1% of the time
where the time goes in v1:
time: 647 us; the launch traced here: 638 us
  Pallas kernels  512 us (79%)
  other arithmetic  75.7 us (12%)
  local copies, waits for them, and re-layouts  29.9 us (5%)
  matrix products  18.7 us (3%)
    pallas_call x1, Pallas kernels, close_call(): pl.pallas_call(functools.partial(close_kernel, shards, reps), out_shape=[...  166 us
    pallas_call x1, Pallas kernels, open_call(): pl.pallas_call(functools.partial(open_kernel, shards, reps), out_shape=sh...  149 us
    pallas_call x1, Pallas kernels, expert_call(): pl.pallas_call(functools.partial(expert_kernel, shards), grid=(2 * BLOCKS...  148 us
    sub x6, other arithmetic, adamw(): return (first_new, second_new, weight - rate * (update + decay * weight))  50.8 us
    pallas_call x1, Pallas kernels, spread_call(): pl.pallas_call(spread_kernel, out_shape=[jax.ShapeDtypeStruct((len(POSITI...  49 us

profile of v1, /device:TPU:0, one launch (start us, length us, event | category | flops | bytes accessed | tf_op | source)
XLA Modules:
  0.0 637.9 jit_solution(7335404403045870773)
XLA Ops:
  0.7 3.4 dynamic-slice_convert_fusion.refs_3_
  4.1 2.4 dynamic-slice_convert_fusion.1.refs_4_
  10.1 148.9 %open_gather.1 = (bf16[8,192,2560]{2,1,0:T(8,128)(2,1)}, bf16[8,192,1536]{2,1,0:T(8,128)(2,1)}, bf16[8,192,128]{2,1,0:T(8,128)(2,1)}, bf16[2,8,192,1024]{3,2,1,0...) custom-call(bf16[192,2560]{1,0:T(8,128)(2,1)} %convert_element_type.96.refs_0_, ...), custom_call_target="tpu_custom_call" | custom-call | tf_op jit(solution)/shard_map/open_gather/pallas_call | solution.py:565
  161.7 5.7 fusion.51
  167.5 1.5 copy-done.11
  168.9 1.2 slice.68
  170.2 1.9 copy.233
  177.8 1.4 exponential_reduce_fusion
  179.2 1.7 copy-done.6
  181.7 4.9 fusion.15
  186.7 1.5 multiply_reduce_fusion.2
  190.7 49.0 %spread_tokens.1 = (bf16[8,256,1536]{2,1,0:T(8,128)(2,1)}, f32[8,16,256]{2,1,0:T(8,128)}) custom-call(bf16[256,1536]{1,0:T(8,128)(2,1)} %copy-done.3, f32[16,256]{1,0:T(8,128)} %copy.239.refs_1_), custom_call_target="tpu_custom_call" | custom-call | tf_op jit(solution)/shard_map/spread_tokens/pallas_call | solution.py:611
  241.0 1.4 copy.241
  242.4 2.7 pad_maximum_fusion.refs_2_
  245.0 147.9 %experts.1 = (bf16[256,1536]{1,0:T(8,128)(2,1)}, bf16[256,1536]{1,0:T(8,128)(2,1)}, bf16[256,128]{1,0:T(8,128)(2,1)}, bf16[1536,1024]{1,0:T(8,128)(2,1)}, bf16[5...) custom-call(bf16[2048,1536]{1,0:T(8,128)(2,1)} %bitcast.78, ...), custom_call_target="tpu_custom_call" | custom-call | tf_op jit(solution)/shard_map/experts/pallas_call | solution.py:945
  395.7 1.6 convolution_convert_fusion
  397.6 3.5 multiply_reduce_fusion
  403.9 2.3 pad_maximum_fusion.1.refs_2_
  406.2 4.1 fusion.49
  413.4 166.1 %close_sums.1 = (bf16[192,2560]{1,0:T(8,128)(2,1)}, bf16[192,1536]{1,0:T(8,128)(2,1)}, bf16[192,128]{1,0:T(8,128)(2,1)}, bf16[16,192,1024]{2,1,0:T(8,128)(2,1)},...) custom-call(bf16[256,1536]{1,0:T(8,128)(2,1)} %get-tuple-element.206, ...), custom_call_target="tpu_custom_call" | custom-call | tf_op jit(solution)/shard_map/close_sums/pallas_call | solution.py:1311
  581.9 30.6 %multiply_subtract_fusion = (f32[16,192,1024]{2,1,0:T(8,128)}, f32[16,192,1024]{2,1,0:T(8,128)}, f32[16,192,1024]{2,1,0:T(8,128)}) fusion(f32[16,192,1024]{2,1,0:T(8,128)} %param.35, bf16[16,192,1024]{2,1,0:T(8,128)(2,1)} %get-tuple-element.81, f32[16,192,1024]{2,1,0:T(8,128)} %param.37, f32[16,192,1024]{2,1,0:T(8,128)} %param.36), kind=kLoop, calls=%fused_computation.4 | loop fusion | flops 50331648 | bytes 81788928 | tf_op jit(solution)/shard_map/sub | solution.py:381
  612.5 14.0 %multiply_subtract_fusion.1 = (f32[16,64,1536]{2,1,0:T(8,128)}, f32[16,64,1536]{2,1,0:T(8,128)}, f32[16,64,1536]{2,1,0:T(8,128)}) fusion(f32[16,64,1536]{2,1,0:T(8,128)} %param.38, bf16[16,64,1536]{2,1,0:T(8,128)(2,1)S(1)} %copy-done.10, f32[16,64,1536]{2,1,0:T(8,128)} %param.40, f32[16,64,1536]{2,1,0:T(8,128)} %param.39), kind=kLoop, calls=%fused_computation.10 | loop fusion | flops 25165824 | bytes 40894464 | tf_op jit(solution)/shard_map/sub | solution.py:381
  626.6 3.6 multiply_subtract_fusion.2
  630.3 2.4 multiply_subtract_fusion.3
  (185 shorter events, 32.6 us)
Async XLA Ops:
  0.7 5.8 copy-start.35
  0.7 6.6 %copy-start.37 = (f32[2,192]{1,0:T(2,128)S(1)}, f32[2,192]{1,0:T(2,128)}, u32[]{:S(2)}) copy-start(f32[2,192]{1,0:T(2,128)} %param.41) | copy-start | bytes 4612
  0.7 7.5 %copy-start.1 = (f32[192,2560]{1,0:T(8,128)S(1)}, f32[192,2560]{1,0:T(8,128)}, u32[]{:S(2)}) copy-start(f32[192,2560]{1,0:T(8,128)} %param.26) | copy-start | bytes 5898244
  161.7 5.8 copy-start.9
  177.8 3.7 copy-start.12
  181.6 5.1 slice-start
  181.7 5.0 slice-start.1
  189.8 50.8 %copy-start.38 = (f32[256]{0:T(256)}, f32[256]{0:T(256)S(1)}, u32[]{:S(2)}) copy-start(f32[256]{0:T(256)S(1)} %fusion.30) | copy-start | bytes 3076
  393.0 4.6 copy-start.17
  393.0 4.6 copy-start.40
  397.6 3.9 copy-start.46
  397.6 4.9 copy-start.19
  397.6 4.9 copy-start.21
  406.2 4.1 copy-start.5
  413.4 166.9 %copy-start.47 = (f32[2,192]{1,0:T(2,128)S(1)}, f32[2,192]{1,0:T(2,128)}, u32[]{:S(2)}) copy-start(f32[2,192]{1,0:T(2,128)} %param.42) | copy-start | bytes 4612
  413.4 167.1 %copy-start.48 = (f32[2,192]{1,0:T(2,128)S(1)}, f32[2,192]{1,0:T(2,128)}, u32[]{:S(2)}) copy-start(f32[2,192]{1,0:T(2,128)} %param.43) | copy-start | bytes 4612
  581.9 30.6 %copy-start.10 = (bf16[16,64,1536]{2,1,0:T(8,128)(2,1)S(1)}, bf16[16,64,1536]{2,1,0:T(8,128)(2,1)}, u32[]{:S(2)}) copy-start(bf16[16,64,1536]{2,1,0:T(8,128)(2,1)} %get-tuple-element.82) | copy-start | bytes 9437188
  612.4 14.1 %copy-start.2 = (f32[192,2560]{1,0:T(8,128)S(1)}, f32[192,2560]{1,0:T(8,128)}, u32[]{:S(2)}) copy-start(f32[192,2560]{1,0:T(8,128)} %param.26) | copy-start | bytes 5898244
  612.5 14.1 %copy-start.13 = (f32[192,2560]{1,0:T(8,128)S(1)}, f32[192,2560]{1,0:T(8,128)}, u32[]{:S(2)}) copy-start(f32[192,2560]{1,0:T(8,128)} %param.28) | copy-start | bytes 5898244
  612.5 14.1 %copy-start.14 = (f32[192,2560]{1,0:T(8,128)S(1)}, f32[192,2560]{1,0:T(8,128)}, u32[]{:S(2)}) copy-start(f32[192,2560]{1,0:T(8,128)} %param.27) | copy-start | bytes 5898244
  612.5 14.1 %copy-start.28 = (bf16[192,2560]{1,0:T(8,128)(2,1)S(1)}, bf16[192,2560]{1,0:T(8,128)(2,1)}, u32[]{:S(2)}) copy-start(bf16[192,2560]{1,0:T(8,128)(2,1)} %get-tuple-element.78) | copy-start | bytes 2949124
  626.6 3.7 copy-start.8
  626.6 3.7 copy-start.26
  632.7 3.9 copy-start.15
  (28 other events, 56.6 us)
